TPU v7x, 256 devices: a whole 4x4x8 slice. The times are simulated.
256 devices in a mesh: ctx: 16 (over x_hi, z), head: 8 (over x_lo, y), rep: 2 (over core).
Axes of the slice: x: 4 (x_hi: 2, x_lo: 2; x = x_hi * 2 + x_lo), y: 4, z: 8, core: 2. Of those that a mesh axis runs over, the one named last changes fastest.
Arguments:
- q_new: bfloat16 [4096, 16384], P(('rep', 'ctx'), 'head'), parts along dimension 0, may hold values from -32 to 32
- k_new: bfloat16 [4096, 1024], P(('rep', 'ctx'), 'head'), parts along dimension 0, may hold values from -6 to 6
- v_new: bfloat16 [4096, 1024], P(('rep', 'ctx'), 'head'), parts along dimension 0, may hold values from -6 to 6
- k_cache: bfloat16 [20480, 1024], P(('rep', 'ctx'), 'head'), parts along dimension 0, may hold values from -32 to 32
- v_cache: bfloat16 [20480, 1024], P(('rep', 'ctx'), 'head'), parts along dimension 0, may hold values from -6 to 6
- new_pos: int32 [4096], P(('rep', 'ctx')), parts along dimension 0, may hold values from 10240 to 12287, as said below
Outputs:
- attended: bfloat16 [4096, 16384], P(('rep', 'ctx'), 'head'), parts along dimension 0
There are 2 independent parts, one for each index of `rep`. A program takes and returns all parts, laid end to end along the dimension named above; each array names one. Nothing has to cross between parts.
Inputs may be any that keep to these rules, and one draw needn't show every extreme that they name: `new_pos`: the new tokens form 2 * 16 blocks of 64 consecutive positions; index d of ctx holds block c and block 31 - c, in this order, for a c that a permutation drawn per request gives; all new positions are 10240 .. 12287, each once.
All inputs are finite; a program needn't handle non-finite values.
Results may differ from a plain program's by a relative error of at most 0.012.
Values may be sent and summed in bfloat16 or wider, within the bound.
A program may use at most 128 MiB of HBM per device.

v0:
```python
import jax
import jax.numpy as jnp
from jax import lax
from jax.sharding import PartitionSpec as P

DH = 128


def passed_along(block, axis, distance):
    devices = range(lax.axis_size(axis))
    route = [((i - distance) % len(devices), i) for i in devices]
    return lax.ppermute(block, axis, route)


def rotate(values_in, positions):
    rows = values_in.shape[0]
    heads = values_in.shape[1] // DH
    half = DH // 2
    grid = values_in.astype(jnp.float32).reshape(rows, heads, DH)
    freqs = 500000.0 ** (-(2.0 * jnp.arange(half, dtype=jnp.float32)) / DH)
    angles = positions.astype(jnp.float32)[:, None] * freqs[None, :]
    cosine = jnp.cos(angles)[:, None, :]
    sine = jnp.sin(angles)[:, None, :]
    lower = grid[..., :half]
    upper = grid[..., half:]
    turned = jnp.concatenate(
        [lower * cosine - upper * sine, upper * cosine + lower * sine], axis=-1
    )
    return turned.reshape(rows, heads * DH).astype(jnp.bfloat16)


def attend_block(queries, query_pos, keys, values, key_pos):
    qrows = queries.shape[0]
    krows = keys.shape[0]
    kv_heads = keys.shape[1] // DH
    q_heads = queries.shape[1] // DH
    group = q_heads // kv_heads
    query_heads = queries.reshape(qrows, kv_heads, group, DH)
    key_heads = keys.reshape(krows, kv_heads, DH)
    value_heads = values.reshape(krows, kv_heads, DH)
    scores = jnp.einsum(
        "qkgd,nkd->kgqn", query_heads, key_heads, preferred_element_type=jnp.float32
    )
    scores = scores * (1.0 / DH**0.5)
    allowed = key_pos[None, :] <= query_pos[:, None]
    scores = jnp.where(allowed[None, None], scores, jnp.float32(-1e30))
    top = jnp.max(scores, axis=-1)
    expo = jnp.exp(scores - top[..., None])
    total = jnp.sum(expo, axis=-1)
    weights = expo.astype(jnp.bfloat16)
    mixed = jnp.einsum("kgqn,nkd->qkgd", weights, value_heads, preferred_element_type=jnp.float32)
    mixed = mixed / jnp.transpose(total, (2, 0, 1))[..., None]
    part_out = mixed.reshape(qrows, q_heads * DH).astype(jnp.bfloat16)
    part_lse = jnp.transpose(top + jnp.log(total), (2, 0, 1)).reshape(qrows, q_heads)
    return (part_out, part_lse)


def combine_partials(outs, lses):
    shards, qrows, heads = lses.shape
    top = jnp.max(lses, axis=0)
    total = top + jnp.log(jnp.sum(jnp.exp(lses - top[None]), axis=0))
    weights = jnp.exp(lses - total[None])
    spread = outs.astype(jnp.float32).reshape(shards, qrows, heads, DH)
    summed = jnp.sum(weights[..., None] * spread, axis=0)
    return summed.reshape(qrows, heads * DH).astype(jnp.bfloat16)


def body(q_new, k_new, v_new, k_cache, v_cache, new_pos):
    index = lax.axis_index("ctx")
    shard_count = lax.axis_size("ctx")
    cache_rows = k_cache.shape[0]
    query_rows = q_new.shape[0]
    key_rows = cache_rows + query_rows
    q_heads = q_new.shape[1] // DH
    q_rot = rotate(q_new, new_pos)
    k_rot = rotate(k_new, new_pos)
    keys_local = jnp.concatenate([k_cache, k_rot], axis=0)
    values_local = jnp.concatenate([v_cache, v_new], axis=0)
    cache_pos = index * cache_rows + jnp.arange(cache_rows, dtype=jnp.int32)
    key_pos = jnp.concatenate([cache_pos, new_pos], axis=0)
    every_pos = lax.all_gather(key_pos, "ctx", axis=0, tiled=True)
    table_pos = every_pos.reshape(shard_count, key_rows)

    def visit_block(step_index, buffers):
        block, out_buffer, lse_buffer = buffers
        anchor = (index - step_index) % shard_count
        block_pos = lax.dynamic_index_in_dim(table_pos, anchor, 0, keepdims=False)[cache_rows:]
        part_out, part_lse = attend_block(block, block_pos, keys_local, values_local, key_pos)
        out_buffer = lax.dynamic_update_index_in_dim(out_buffer, part_out, anchor, 0)
        lse_buffer = lax.dynamic_update_index_in_dim(lse_buffer, part_lse, anchor, 0)
        block = passed_along(block, "ctx", 1)
        return (block, out_buffer, lse_buffer)

    start_out = jnp.zeros((shard_count, query_rows, q_new.shape[1]), jnp.bfloat16)
    start_lse = jnp.zeros((shard_count, query_rows, q_heads), jnp.float32)
    block, out_buffer, lse_buffer = lax.fori_loop(
        0, shard_count - 1, visit_block, (q_rot, start_out, start_lse)
    )
    anchor = (index + 1) % shard_count
    block_pos = lax.dynamic_index_in_dim(table_pos, anchor, 0, keepdims=False)[cache_rows:]
    part_out, part_lse = attend_block(block, block_pos, keys_local, values_local, key_pos)
    out_buffer = lax.dynamic_update_index_in_dim(out_buffer, part_out, anchor, 0)
    lse_buffer = lax.dynamic_update_index_in_dim(lse_buffer, part_lse, anchor, 0)
    got_out = lax.all_to_all(out_buffer, "ctx", split_axis=0, concat_axis=0, tiled=True)
    got_lse = lax.all_to_all(lse_buffer, "ctx", split_axis=0, concat_axis=0, tiled=True)
    return combine_partials(got_out, got_lse)


def solution(mesh):
    in_specs = (
        P(("rep", "ctx"), "head"),
        P(("rep", "ctx"), "head"),
        P(("rep", "ctx"), "head"),
        P(("rep", "ctx"), "head"),
        P(("rep", "ctx"), "head"),
        P(("rep", "ctx")),
    )
    out_specs = P(("rep", "ctx"), "head")
    return jax.shard_map(body, mesh=mesh, in_specs=in_specs, out_specs=out_specs, check_vma=False)
```

profile of v0, /device:TPU:8, one launch (start us, length us, event | category | flops | bytes accessed | tf_op | source)
XLA Modules:
  0.0 477.3 jit_solution(8825735547021509342)
XLA Ops:
  0.1 1.2 convert_bitcast_fusion
  3.5 44.1 %all-gather = s32[16,1,768]{2,1,0:T(1,128)S(1)} all-gather(s32[1,1,768]{2,1,0:T(1,128)S(1)} %reshape.381), channel_id=1, replica_groups=mesh['ctx'=16,'head'=8,'rep'=2] {'ctx'}, dimensions={0}, use_global_device_ids=true | all-gather | bytes 52224 | tf_op jit(solution)/shard_map/all_gather | solution.py:81
  48.6 4.8 %broadcast_in_dim.94 = bf16[16,128,2048]{1,2,0:T(8,128)(2,1)} broadcast(bf16[]{:T(256)} %constant.126.clone.1), dimensions={} | broadcast | bytes 8388610 | tf_op jit(solution)/shard_map/broadcast_in_dim | solution.py:94
  54.2 228.2 %while.19 = (s32[]{:T(128)}, bf16[128,2048]{1,0:T(8,128)(2,1)S(1)}, bf16[16,128,2048]{1,2,0:T(8,128)(2,1)}, f32[16,128,16]{1,2,0:T(8,128)}, s32[768]{0:T(1024)S(...) while((s32[]{:T(128)}, bf16[128,2048]{1,0:T(8,128)(2,1)S(1)}, ...), condition=%wide.region_3.4_spmd, body=%wide.region_0.3_spmd.sunk | while | flops 823228416 | bytes 24974180 | solution.py:96
  55.6 1.3 fusion.59
  57.0 1.7 divide_convert_fusion.3
  60.1 9.1 %collective-permute-done = bf16[128,2048]{1,0:T(8,128)(2,1)S(1)} collective-permute-done((bf16[128,2048]{1,0:T(8,128)(2,1)S(1)}, bf16[128,2048]{1,0:T(8,128)(2,1)S(1)}, u32[]{:S(2)}, u32[]{:S(2)}) %collective-permute-start) | collective-permute-done | bytes 524320 | tf_op jit(solution)/shard_map/while/body/eval_jaxpr/ppermute | solution.py:12
  69.6 1.1 fusion.58
  70.7 1.3 fusion.59
  72.0 1.7 divide_convert_fusion.3
  75.2 10.2 %collective-permute-done = bf16[128,2048]{1,0:T(8,128)(2,1)S(1)} collective-permute-done((bf16[128,2048]{1,0:T(8,128)(2,1)S(1)}, bf16[128,2048]{1,0:T(8,128)(2,1)S(1)}, u32[]{:S(2)}, u32[]{:S(2)}) %collective-permute-start) | collective-permute-done | bytes 524320 | tf_op jit(solution)/shard_map/while/body/eval_jaxpr/ppermute | solution.py:12
  86.8 1.3 fusion.59
  88.2 1.7 divide_convert_fusion.3
  91.3 11.3 %collective-permute-done = bf16[128,2048]{1,0:T(8,128)(2,1)S(1)} collective-permute-done((bf16[128,2048]{1,0:T(8,128)(2,1)S(1)}, bf16[128,2048]{1,0:T(8,128)(2,1)S(1)}, u32[]{:S(2)}, u32[]{:S(2)}) %collective-permute-start) | collective-permute-done | bytes 524320 | tf_op jit(solution)/shard_map/while/body/eval_jaxpr/ppermute | solution.py:12
  104.1 1.3 fusion.59
  105.4 1.7 divide_convert_fusion.3
  108.6 12.4 %collective-permute-done = bf16[128,2048]{1,0:T(8,128)(2,1)S(1)} collective-permute-done((bf16[128,2048]{1,0:T(8,128)(2,1)S(1)}, bf16[128,2048]{1,0:T(8,128)(2,1)S(1)}, u32[]{:S(2)}, u32[]{:S(2)}) %collective-permute-start) | collective-permute-done | bytes 524320 | tf_op jit(solution)/shard_map/while/body/eval_jaxpr/ppermute | solution.py:12
  121.5 1.1 fusion.58
  122.5 1.3 fusion.59
  123.9 1.7 divide_convert_fusion.3
  127.0 11.7 %collective-permute-done = bf16[128,2048]{1,0:T(8,128)(2,1)S(1)} collective-permute-done((bf16[128,2048]{1,0:T(8,128)(2,1)S(1)}, bf16[128,2048]{1,0:T(8,128)(2,1)S(1)}, u32[]{:S(2)}, u32[]{:S(2)}) %collective-permute-start) | collective-permute-done | bytes 524320 | tf_op jit(solution)/shard_map/while/body/eval_jaxpr/ppermute | solution.py:12
  140.2 1.3 fusion.59
  141.5 1.7 divide_convert_fusion.3
  144.7 10.9 %collective-permute-done = bf16[128,2048]{1,0:T(8,128)(2,1)S(1)} collective-permute-done((bf16[128,2048]{1,0:T(8,128)(2,1)S(1)}, bf16[128,2048]{1,0:T(8,128)(2,1)S(1)}, u32[]{:S(2)}, u32[]{:S(2)}) %collective-permute-start) | collective-permute-done | bytes 524320 | tf_op jit(solution)/shard_map/while/body/eval_jaxpr/ppermute | solution.py:12
  156.0 1.1 fusion.58
  157.0 1.3 fusion.59
  158.4 1.7 divide_convert_fusion.3
  161.5 10.0 %collective-permute-done = bf16[128,2048]{1,0:T(8,128)(2,1)S(1)} collective-permute-done((bf16[128,2048]{1,0:T(8,128)(2,1)S(1)}, bf16[128,2048]{1,0:T(8,128)(2,1)S(1)}, u32[]{:S(2)}, u32[]{:S(2)}) %collective-permute-start) | collective-permute-done | bytes 524320 | tf_op jit(solution)/shard_map/while/body/eval_jaxpr/ppermute | solution.py:12
  173.0 1.3 fusion.59
  174.3 1.7 divide_convert_fusion.3
  177.5 9.0 %collective-permute-done = bf16[128,2048]{1,0:T(8,128)(2,1)S(1)} collective-permute-done((bf16[128,2048]{1,0:T(8,128)(2,1)S(1)}, bf16[128,2048]{1,0:T(8,128)(2,1)S(1)}, u32[]{:S(2)}, u32[]{:S(2)}) %collective-permute-start) | collective-permute-done | bytes 524320 | tf_op jit(solution)/shard_map/while/body/eval_jaxpr/ppermute | solution.py:12
  188.0 1.3 fusion.59
  189.3 1.7 divide_convert_fusion.3
  192.4 8.1 %collective-permute-done = bf16[128,2048]{1,0:T(8,128)(2,1)S(1)} collective-permute-done((bf16[128,2048]{1,0:T(8,128)(2,1)S(1)}, bf16[128,2048]{1,0:T(8,128)(2,1)S(1)}, u32[]{:S(2)}, u32[]{:S(2)}) %collective-permute-start) | collective-permute-done | bytes 524320 | tf_op jit(solution)/shard_map/while/body/eval_jaxpr/ppermute | solution.py:12
  201.0 1.1 fusion.58
  202.0 1.3 fusion.59
  203.4 1.7 divide_convert_fusion.3
  206.5 7.2 %collective-permute-done = bf16[128,2048]{1,0:T(8,128)(2,1)S(1)} collective-permute-done((bf16[128,2048]{1,0:T(8,128)(2,1)S(1)}, bf16[128,2048]{1,0:T(8,128)(2,1)S(1)}, u32[]{:S(2)}, u32[]{:S(2)}) %collective-permute-start) | collective-permute-done | bytes 524320 | tf_op jit(solution)/shard_map/while/body/eval_jaxpr/ppermute | solution.py:12
  215.2 1.3 fusion.59
  216.5 1.7 divide_convert_fusion.3
  219.7 7.1 %collective-permute-done = bf16[128,2048]{1,0:T(8,128)(2,1)S(1)} collective-permute-done((bf16[128,2048]{1,0:T(8,128)(2,1)S(1)}, bf16[128,2048]{1,0:T(8,128)(2,1)S(1)}, u32[]{:S(2)}, u32[]{:S(2)}) %collective-permute-start) | collective-permute-done | bytes 524320 | tf_op jit(solution)/shard_map/while/body/eval_jaxpr/ppermute | solution.py:12
  227.1 1.1 fusion.58
  228.2 1.3 fusion.59
  229.5 1.7 divide_convert_fusion.3
  232.7 8.1 %collective-permute-done = bf16[128,2048]{1,0:T(8,128)(2,1)S(1)} collective-permute-done((bf16[128,2048]{1,0:T(8,128)(2,1)S(1)}, bf16[128,2048]{1,0:T(8,128)(2,1)S(1)}, u32[]{:S(2)}, u32[]{:S(2)}) %collective-permute-start) | collective-permute-done | bytes 524320 | tf_op jit(solution)/shard_map/while/body/eval_jaxpr/ppermute | solution.py:12
  241.2 1.1 fusion.58
  242.3 1.3 fusion.59
  243.6 1.7 divide_convert_fusion.3
  246.7 9.2 %collective-permute-done = bf16[128,2048]{1,0:T(8,128)(2,1)S(1)} collective-permute-done((bf16[128,2048]{1,0:T(8,128)(2,1)S(1)}, bf16[128,2048]{1,0:T(8,128)(2,1)S(1)}, u32[]{:S(2)}, u32[]{:S(2)}) %collective-permute-start) | collective-permute-done | bytes 524320 | tf_op jit(solution)/shard_map/while/body/eval_jaxpr/ppermute | solution.py:12
  257.4 1.3 fusion.59
  258.7 1.7 divide_convert_fusion.3
  261.9 7.0 %collective-permute-done = bf16[128,2048]{1,0:T(8,128)(2,1)S(1)} collective-permute-done((bf16[128,2048]{1,0:T(8,128)(2,1)S(1)}, bf16[128,2048]{1,0:T(8,128)(2,1)S(1)}, u32[]{:S(2)}, u32[]{:S(2)}) %collective-permute-start) | collective-permute-done | bytes 524320 | tf_op jit(solution)/shard_map/while/body/eval_jaxpr/ppermute | solution.py:12
  269.3 1.1 fusion.58
  270.3 1.3 fusion.59
  271.7 1.7 divide_convert_fusion.3
  274.8 7.6 %collective-permute-done = bf16[128,2048]{1,0:T(8,128)(2,1)S(1)} collective-permute-done((bf16[128,2048]{1,0:T(8,128)(2,1)S(1)}, bf16[128,2048]{1,0:T(8,128)(2,1)S(1)}, u32[]{:S(2)}, u32[]{:S(2)}) %collective-permute-start) | collective-permute-done | bytes 524320 | tf_op jit(solution)/shard_map/while/body/eval_jaxpr/ppermute | solution.py:12
  283.4 2.7 copy-done
  286.2 1.3 fusion.21
  288.1 3.7 all-to-all-start
  291.8 4.4 divide_convert_fusion.1
  297.1 5.9 %all-to-all-done = f32[16,128,16]{1,2,0:T(8,128)S(1)} async-done(((f32[16,128,16]{1,2,0:T(8,128)}), f32[16,128,16]{1,2,0:T(8,128)S(1)}, u32[]{:S(2)}, u32[]{:S(2)}) %all-to-all-start) | async-done | bytes 131104 | tf_op jit(solution)/shard_map/all_to_all | solution.py:105
  303.0 6.3 %all-to-all-start.1 = ((bf16[16,128,2048]{1,2,0:T(8,128)(2,1)}), bf16[16,128,2048]{1,2,0:T(8,128)(2,1)}, u32[]{:S(2)}, u32[]{:S(2)}) async-start(bf16[16,128,2048]{1,2,0:T(8,128)(2,1)} %constant_dynamic-update-slice_fusion.1), calls=%async_computation.1 | async-start | bytes 16777216 | tf_op jit(solution)/shard_map/all_to_all | solution.py:104
  309.4 161.8 %all-to-all-done.1 = bf16[16,128,2048]{1,2,0:T(8,128)(2,1)} async-done(((bf16[16,128,2048]{1,2,0:T(8,128)(2,1)}), bf16[16,128,2048]{1,2,0:T(8,128)(2,1)}, u32[]{:S(2)}, u32[]{:S(2)}) %all-to-all-start.1) | async-done | bytes 8388640 | tf_op jit(solution)/shard_map/all_to_all | solution.py:104
  471.2 5.0 %fusion.19 = bf16[128,2048]{0,1:T(8,128)(2,1)S(1)} fusion(bf16[16,128,2048]{1,2,0:T(8,128)(2,1)} %all-to-all-done.1, f32[16,128,16]{1,2,0:T(8,128)S(1)} %subtract_exponential_fusion.2), kind=kLoop, calls=%fused_computation.24 | loop fusion | flops 12320768 | bytes 9043968 | tf_op jit(solution)/shard_map/reduce_sum | solution.py:64
  (141 shorter events, 43.1 us)
Async XLA Ops:
  0.0 3.5 copy-start.5
  0.0 47.6 %copy-start.3 = (bf16[128,128]{1,0:T(8,128)(2,1)S(1)}, bf16[128,128]{1,0:T(8,128)(2,1)}, u32[]{:S(2)}) copy-start(bf16[128,128]{1,0:T(8,128)(2,1)} %param.9) | copy-start | bytes 98308
  0.0 48.1 %copy-start.4 = (bf16[128,128]{1,0:T(8,128)(2,1)S(1)}, bf16[128,128]{1,0:T(8,128)(2,1)}, u32[]{:S(2)}) copy-start(bf16[128,128]{1,0:T(8,128)(2,1)} %param.10) | copy-start | bytes 98308
  0.0 48.2 %copy-start.2 = (bf16[640,128]{1,0:T(8,128)(2,1)S(1)}, bf16[640,128]{1,0:T(8,128)(2,1)}, u32[]{:S(2)}) copy-start(bf16[640,128]{1,0:T(8,128)(2,1)} %param.12) | copy-start | bytes 491524
  0.0 48.6 %copy-start.1 = (bf16[640,128]{1,0:T(8,128)(2,1)S(1)}, bf16[640,128]{1,0:T(8,128)(2,1)}, u32[]{:S(2)}) copy-start(bf16[640,128]{1,0:T(8,128)(2,1)} %param.11) | copy-start | bytes 491524
  54.2 15.0 %collective-permute-start = (bf16[128,2048]{1,0:T(8,128)(2,1)S(1)}, bf16[128,2048]{1,0:T(8,128)(2,1)S(1)}, u32[]{:S(2)}, u32[]{:S(2)}) collective-permute-start(bf16[128,2048]{1,0:T(8,128)(2,1)S(1)} %copy.61), channel_id=1, source_target_pairs={{240,0},{0,16},{16,32},{32,48},{48,64},{64,80},{80,96},{96,112},{1... | collective-permute-start | bytes 1572872 | tf_op jit(solution)/shard_map/while/body/eval_jaxpr/ppermute | solution.py:12
  69.3 16.1 %collective-permute-start = (bf16[128,2048]{1,0:T(8,128)(2,1)S(1)}, bf16[128,2048]{1,0:T(8,128)(2,1)S(1)}, u32[]{:S(2)}, u32[]{:S(2)}) collective-permute-start(bf16[128,2048]{1,0:T(8,128)(2,1)S(1)} %copy.61), channel_id=1, source_target_pairs={{240,0},{0,16},{16,32},{32,48},{48,64},{64,80},{80,96},{96,112},{1... | collective-permute-start | bytes 1572872 | tf_op jit(solution)/shard_map/while/body/eval_jaxpr/ppermute | solution.py:12
  85.4 17.2 %collective-permute-start = (bf16[128,2048]{1,0:T(8,128)(2,1)S(1)}, bf16[128,2048]{1,0:T(8,128)(2,1)S(1)}, u32[]{:S(2)}, u32[]{:S(2)}) collective-permute-start(bf16[128,2048]{1,0:T(8,128)(2,1)S(1)} %copy.61), channel_id=1, source_target_pairs={{240,0},{0,16},{16,32},{32,48},{48,64},{64,80},{80,96},{96,112},{1... | collective-permute-start | bytes 1572872 | tf_op jit(solution)/shard_map/while/body/eval_jaxpr/ppermute | solution.py:12
  102.7 18.4 %collective-permute-start = (bf16[128,2048]{1,0:T(8,128)(2,1)S(1)}, bf16[128,2048]{1,0:T(8,128)(2,1)S(1)}, u32[]{:S(2)}, u32[]{:S(2)}) collective-permute-start(bf16[128,2048]{1,0:T(8,128)(2,1)S(1)} %copy.61), channel_id=1, source_target_pairs={{240,0},{0,16},{16,32},{32,48},{48,64},{64,80},{80,96},{96,112},{1... | collective-permute-start | bytes 1572872 | tf_op jit(solution)/shard_map/while/body/eval_jaxpr/ppermute | solution.py:12
  121.1 17.6 %collective-permute-start = (bf16[128,2048]{1,0:T(8,128)(2,1)S(1)}, bf16[128,2048]{1,0:T(8,128)(2,1)S(1)}, u32[]{:S(2)}, u32[]{:S(2)}) collective-permute-start(bf16[128,2048]{1,0:T(8,128)(2,1)S(1)} %copy.61), channel_id=1, source_target_pairs={{240,0},{0,16},{16,32},{32,48},{48,64},{64,80},{80,96},{96,112},{1... | collective-permute-start | bytes 1572872 | tf_op jit(solution)/shard_map/while/body/eval_jaxpr/ppermute | solution.py:12
  138.8 16.8 %collective-permute-start = (bf16[128,2048]{1,0:T(8,128)(2,1)S(1)}, bf16[128,2048]{1,0:T(8,128)(2,1)S(1)}, u32[]{:S(2)}, u32[]{:S(2)}) collective-permute-start(bf16[128,2048]{1,0:T(8,128)(2,1)S(1)} %copy.61), channel_id=1, source_target_pairs={{240,0},{0,16},{16,32},{32,48},{48,64},{64,80},{80,96},{96,112},{1... | collective-permute-start | bytes 1572872 | tf_op jit(solution)/shard_map/while/body/eval_jaxpr/ppermute | solution.py:12
  155.6 15.9 %collective-permute-start = (bf16[128,2048]{1,0:T(8,128)(2,1)S(1)}, bf16[128,2048]{1,0:T(8,128)(2,1)S(1)}, u32[]{:S(2)}, u32[]{:S(2)}) collective-permute-start(bf16[128,2048]{1,0:T(8,128)(2,1)S(1)} %copy.61), channel_id=1, source_target_pairs={{240,0},{0,16},{16,32},{32,48},{48,64},{64,80},{80,96},{96,112},{1... | collective-permute-start | bytes 1572872 | tf_op jit(solution)/shard_map/while/body/eval_jaxpr/ppermute | solution.py:12
  171.5 15.0 %collective-permute-start = (bf16[128,2048]{1,0:T(8,128)(2,1)S(1)}, bf16[128,2048]{1,0:T(8,128)(2,1)S(1)}, u32[]{:S(2)}, u32[]{:S(2)}) collective-permute-start(bf16[128,2048]{1,0:T(8,128)(2,1)S(1)} %copy.61), channel_id=1, source_target_pairs={{240,0},{0,16},{16,32},{32,48},{48,64},{64,80},{80,96},{96,112},{1... | collective-permute-start | bytes 1572872 | tf_op jit(solution)/shard_map/while/body/eval_jaxpr/ppermute | solution.py:12
  186.5 14.0 %collective-permute-start = (bf16[128,2048]{1,0:T(8,128)(2,1)S(1)}, bf16[128,2048]{1,0:T(8,128)(2,1)S(1)}, u32[]{:S(2)}, u32[]{:S(2)}) collective-permute-start(bf16[128,2048]{1,0:T(8,128)(2,1)S(1)} %copy.61), channel_id=1, source_target_pairs={{240,0},{0,16},{16,32},{32,48},{48,64},{64,80},{80,96},{96,112},{1... | collective-permute-start | bytes 1572872 | tf_op jit(solution)/shard_map/while/body/eval_jaxpr/ppermute | solution.py:12
  200.6 13.1 %collective-permute-start = (bf16[128,2048]{1,0:T(8,128)(2,1)S(1)}, bf16[128,2048]{1,0:T(8,128)(2,1)S(1)}, u32[]{:S(2)}, u32[]{:S(2)}) collective-permute-start(bf16[128,2048]{1,0:T(8,128)(2,1)S(1)} %copy.61), channel_id=1, source_target_pairs={{240,0},{0,16},{16,32},{32,48},{48,64},{64,80},{80,96},{96,112},{1... | collective-permute-start | bytes 1572872 | tf_op jit(solution)/shard_map/while/body/eval_jaxpr/ppermute | solution.py:12
  213.8 13.0 %collective-permute-start = (bf16[128,2048]{1,0:T(8,128)(2,1)S(1)}, bf16[128,2048]{1,0:T(8,128)(2,1)S(1)}, u32[]{:S(2)}, u32[]{:S(2)}) collective-permute-start(bf16[128,2048]{1,0:T(8,128)(2,1)S(1)} %copy.61), channel_id=1, source_target_pairs={{240,0},{0,16},{16,32},{32,48},{48,64},{64,80},{80,96},{96,112},{1... | collective-permute-start | bytes 1572872 | tf_op jit(solution)/shard_map/while/body/eval_jaxpr/ppermute | solution.py:12
  226.8 14.0 %collective-permute-start = (bf16[128,2048]{1,0:T(8,128)(2,1)S(1)}, bf16[128,2048]{1,0:T(8,128)(2,1)S(1)}, u32[]{:S(2)}, u32[]{:S(2)}) collective-permute-start(bf16[128,2048]{1,0:T(8,128)(2,1)S(1)} %copy.61), channel_id=1, source_target_pairs={{240,0},{0,16},{16,32},{32,48},{48,64},{64,80},{80,96},{96,112},{1... | collective-permute-start | bytes 1572872 | tf_op jit(solution)/shard_map/while/body/eval_jaxpr/ppermute | solution.py:12
  240.8 15.1 %collective-permute-start = (bf16[128,2048]{1,0:T(8,128)(2,1)S(1)}, bf16[128,2048]{1,0:T(8,128)(2,1)S(1)}, u32[]{:S(2)}, u32[]{:S(2)}) collective-permute-start(bf16[128,2048]{1,0:T(8,128)(2,1)S(1)} %copy.61), channel_id=1, source_target_pairs={{240,0},{0,16},{16,32},{32,48},{48,64},{64,80},{80,96},{96,112},{1... | collective-permute-start | bytes 1572872 | tf_op jit(solution)/shard_map/while/body/eval_jaxpr/ppermute | solution.py:12
  256.0 12.9 %collective-permute-start = (bf16[128,2048]{1,0:T(8,128)(2,1)S(1)}, bf16[128,2048]{1,0:T(8,128)(2,1)S(1)}, u32[]{:S(2)}, u32[]{:S(2)}) collective-permute-start(bf16[128,2048]{1,0:T(8,128)(2,1)S(1)} %copy.61), channel_id=1, source_target_pairs={{240,0},{0,16},{16,32},{32,48},{48,64},{64,80},{80,96},{96,112},{1... | collective-permute-start | bytes 1572872 | tf_op jit(solution)/shard_map/while/body/eval_jaxpr/ppermute | solution.py:12
  268.9 13.5 %collective-permute-start = (bf16[128,2048]{1,0:T(8,128)(2,1)S(1)}, bf16[128,2048]{1,0:T(8,128)(2,1)S(1)}, u32[]{:S(2)}, u32[]{:S(2)}) collective-permute-start(bf16[128,2048]{1,0:T(8,128)(2,1)S(1)} %copy.61), channel_id=1, source_target_pairs={{240,0},{0,16},{16,32},{32,48},{48,64},{64,80},{80,96},{96,112},{1... | collective-permute-start | bytes 1572872 | tf_op jit(solution)/shard_map/while/body/eval_jaxpr/ppermute | solution.py:12
  283.4 2.7 copy-start
  288.1 14.9 %all-to-all-start = ((f32[16,128,16]{1,2,0:T(8,128)}), f32[16,128,16]{1,2,0:T(8,128)S(1)}, u32[]{:S(2)}, u32[]{:S(2)}) async-start(f32[16,128,16]{1,2,0:T(8,128)} %bitcast_dynamic-update-slice_fusion.1), calls=%async_computation | async-start | bytes 262144 | tf_op jit(solution)/shard_map/all_to_all | solution.py:105
  303.0 168.2 %all-to-all-start.1 = ((bf16[16,128,2048]{1,2,0:T(8,128)(2,1)}), bf16[16,128,2048]{1,2,0:T(8,128)(2,1)}, u32[]{:S(2)}, u32[]{:S(2)}) async-start(bf16[16,128,2048]{1,2,0:T(8,128)(2,1)} %constant_dynamic-update-slice_fusion.1), calls=%async_computation.1 | async-start | bytes 16777216 | tf_op jit(solution)/shard_map/all_to_all | solution.py:104
where the time goes:
time: 478 us; the launch traced here: 477 us
  waiting for transfers between devices  307 us (64%)
  matrix products  46.7 us (10%)
  blocking collectives  44.1 us (9%)
  other arithmetic  42.1 us (9%)
  local copies, waits for them, and re-layouts  25.2 us (5%)
  starting transfers between devices  11.2 us (2%)
    all_to_all x1, waiting for transfers between devices, body(): lax.all_to_all(out_buffer, 'ctx', split_axis=0, concat_axis=0, tiled=True)  162 us
    ppermute x15, waiting for transfers between devices, passed_along(): return lax.ppermute(block, axis, route)  139 us
    all_gather x1, blocking collectives, body(): every_pos = lax.all_gather(key_pos, 'ctx', axis=0, tiled=True)  44.1 us
    dot_general x16, matrix products, attend_block(): jnp.einsum('kgqn,nkd->qkgd', weights, value_heads, preferred_element_type...  29.9 us
    reduce_sum x16, other arithmetic, attend_block(): total = jnp.sum(expo, axis=-1)  21.1 us
    dot_general x16, matrix products, attend_block(): jnp.einsum('qkgd,nkd->kgqn', query_heads, key_heads, preferred_element_ty...  16.9 us
    dynamic_update_slice x15, local copies, waits for them, and re-layouts, visit_block(): lax.dynamic_update_index_in_dim(out_buffer, part_out, anchor, 0)  12.6 us
  transfers between devices with their start and end apart: 17, of which 17 were waited for; matrix products, arithmetic and copies ran while one was open for 19% of the time, Pallas kernels for 0%

commit v1 on v0

v1 whole, which is shorter than its diff:
```python
import functools
import math

import jax
import jax.numpy as jnp
import numpy as np
from jax import lax
from jax.experimental import pallas as pl
from jax.experimental.pallas import tpu as pltpu
from jax.sharding import PartitionSpec as P

DH = 128
HALF = 64
F32 = jnp.float32
BF16 = jnp.bfloat16
MESH = pl.DeviceIdType.MESH
LOG2E = math.log2(math.e)
SCALE = LOG2E / math.sqrt(DH)
NEG = -1e30
CACHED = 10240

ZN = 8
PART = 384
OLD = 320
ROWS = 2 * PART + 16
QB = 512
NQB = 4
CB = 1024
NCB = 2
OROWS = DH + 16
EARLY = 3
UNITS = 2 * ZN


def mm(a, b):
    return lax.dot_general(
        a, b, (((1,), (0,)), ((), ())), preferred_element_type=F32
    )


def turn(x, cosine, sine):
    lower, upper = x[:HALF], x[HALF:]
    return jnp.concatenate(
        [lower * cosine - upper * sine, upper * cosine + lower * sine], axis=0
    )


def kernel(
    ny, q_ref, kn_ref, vn_ref, kc_ref, vc_ref, pos_ref, freq_ref, out_ref,
    qt, fq, kv, qp, acc, top, s0, s1, x0, x1, so, fo, ro,
    kv_send, kv_recv, q1_send, q1_recv, q2_send, q2_recv,
    o1_send, o1_recv, o2_send, o2_recv, p_send, p_recv,
):
    ctx = lax.axis_index("ctx")
    head = lax.axis_index("head")
    hi, z = ctx // ZN, ctx % ZN
    lo, y = head // ny, head % ny
    right = {"ctx": hi * ZN + (z + 1) % ZN, "head": head}
    left = {"ctx": hi * ZN + (z + ZN - 1) % ZN, "head": head}
    side_a = {"ctx": ctx, "head": (1 - lo) * ny + y}
    side_b = {"ctx": (1 - hi) * ZN + z, "head": (1 - lo) * ny + y}
    partner = {"ctx": (1 - hi) * ZN + z, "head": head}
    everyone = (right, left, side_a, side_b, partner)

    barrier = pltpu.get_barrier_semaphore()
    for other in everyone:
        pl.semaphore_signal(barrier, inc=1, device_id=other, device_id_type=MESH)

    def remote(src, dst, send, recv, target):
        return pltpu.make_async_remote_copy(
            src_ref=src, dst_ref=dst, send_sem=send, recv_sem=recv,
            device_id=target, device_id_type=MESH,
        )

    def kv_copy(d, s):
        if s <= 2:
            src = kv.at[0, (s - 1) if d == 0 else (2 - s)]
        else:
            src = kv.at[s - 2, d]
        return remote(
            src, kv.at[s, d], kv_send.at[d, s - 1], kv_recv.at[d, s - 1],
            right if d == 0 else left,
        )

    def q_first(b):
        return remote(
            qt.at[0, b], fq.at[b], q1_send.at[b], q1_recv.at[b],
            side_a if b % 2 == 0 else side_b,
        )

    def q_second(b):
        return remote(
            fq.at[b], qt.at[1, b], q2_send.at[b], q2_recv.at[b],
            side_b if b % 2 == 0 else side_a,
        )

    def o_first(b):
        return remote(
            so.at[b], fo.at[b], o1_send.at[b], o1_recv.at[b],
            side_a if b % 2 == 0 else side_b,
        )

    def o_second(b):
        return remote(
            fo.at[b], ro.at[b], o2_send.at[b], o2_recv.at[b],
            side_b if b % 2 == 0 else side_a,
        )

    p_copy = remote(qp.at[0], qp.at[1], p_send, p_recv, partner)

    relative = pos_ref[...].astype(F32) - CACHED
    angle = freq_ref[...] * pos_ref[...].astype(F32)
    cosine, sine = jnp.cos(angle), jnp.sin(angle)
    k_rot = turn(kn_ref[...].astype(F32).T, cosine, sine).T.astype(BF16)
    for d in range(2):
        kv[0, d, 0:OLD, :] = kc_ref[d * OLD:(d + 1) * OLD, :]
        kv[0, d, OLD:PART, :] = k_rot[d * HALF:(d + 1) * HALF]
        v = jnp.concatenate(
            [vc_ref[d * OLD:(d + 1) * OLD, :], vn_ref[d * HALF:(d + 1) * HALF, :]], axis=0
        ).astype(F32)
        for t in range(3):
            kv[0, d, PART + DH * t:PART + DH * (t + 1), :] = (
                v[DH * t:DH * (t + 1)].T.astype(BF16)
            )
        number = relative[:, d * HALF:d * HALF + 1] * (1.0 / HALF)
        kv[0, d, 2 * PART:ROWS, :] = jnp.broadcast_to(number, (16, DH)).astype(BF16)
    qp[0] = jnp.broadcast_to(relative, (8, DH))

    pl.semaphore_wait(barrier, len(everyone))
    for s in (1, 2):
        for d in range(2):
            kv_copy(d, s).start()
    p_copy.start()
    for b in range(NQB):
        for h in range(QB // DH):
            c = b * QB + h * DH
            x = q_ref[:, c:c + DH].astype(F32).T
            qt[0, b, :, h * DH:(h + 1) * DH] = turn(x, cosine, sine).astype(BF16)
        q_first(b).start()
    acc[...] = jnp.zeros(acc.shape, F32)
    top[...] = jnp.full(top.shape, NEG, F32)

    def unit(u):
        group = jnp.where((u >= EARLY) & (u < EARLY + ZN), 1, 0)
        step = jnp.where(u < EARLY, u, jnp.where(u < EARLY + ZN, u - EARLY, u - ZN))
        return group, step

    def score(u, blk, s_ref, x_ref):
        group, step = unit(u)
        q = jnp.concatenate([qt[group, 2 * blk], qt[group, 2 * blk + 1]], axis=1)
        qpos = qp[group][0:1]
        best = None
        for d in range(2):
            s = mm(kv[step, d, 0:PART, :], q) * SCALE
            number = kv[step, d, 2 * PART:ROWS, :].astype(F32)[0:1]
            kpos = number * HALF + lax.broadcasted_iota(jnp.int32, (HALF, DH), 0).astype(F32)
            bias = jnp.where(kpos <= qpos, 0.0, NEG)
            fresh = s[OLD:] + jnp.concatenate([bias] * (CB // DH), axis=1)
            s_ref[d * PART:d * PART + OLD, :] = s[:OLD]
            s_ref[d * PART + OLD:(d + 1) * PART, :] = fresh
            m = jnp.maximum(
                jnp.max(s[:OLD], axis=0, keepdims=True),
                jnp.max(fresh, axis=0, keepdims=True),
            )
            best = m if best is None else jnp.maximum(best, m)
        x_ref[...] = best

    def mix(u, blk, s_ref, x_ref):
        group, step = unit(u)
        before = top[group, blk]
        after = jnp.maximum(before, x_ref[...])
        top[group, blk] = after
        fade = jnp.exp2(before - after)
        p = jnp.exp2(s_ref[...] - after).astype(BF16)
        v = jnp.concatenate(
            [
                kv[step, d, PART + DH * t:PART + DH * (t + 1), :]
                for d in range(2) for t in range(3)
            ],
            axis=1,
        )
        v = jnp.concatenate([v, jnp.ones((16, 2 * PART), BF16)], axis=0)
        acc[group, blk] = acc[group, blk] * fade + mm(v, p)

    def kv_arrive(s):
        for d in range(2):
            kv_copy(d, s).wait_recv()
            if s + 2 < ZN:
                kv_copy(d, s + 2).start()

    def q_pass(b):
        q_first(b).wait_recv()
        q_second(b).start()

    def o_pass(b):
        o_first(b).wait_recv()
        o_second(b).start()

    def partials(group, b):
        blk, c = b // 2, (b % 2) * QB
        a = acc[group, blk, :, c:c + QB]
        total = a[DH:DH + 1]
        lse = top[group, blk, :, c:c + QB] + jnp.log(total) * LOG2E
        return a[:DH] / total, lse

    def after_first(u):
        @pl.when(u == 0)
        def _():
            kv_arrive(1)
            q_pass(0)
            q_pass(1)

        @pl.when(u == 1)
        def _():
            kv_arrive(2)
            q_pass(2)
            q_pass(3)

        @pl.when(u == 2)
        def _():
            p_copy.wait_recv()
            for b in range(NQB):
                q_second(b).wait_recv()

        for at, s in ((3, 3), (4, 4), (6, 5), (8, 6), (9, 7)):
            @pl.when(u == at)
            def _(s=s):
                kv_arrive(s)

        for at, b in ((12, 0), (13, 2)):
            @pl.when(u == at)
            def _(b=b):
                o_pass(b)
                o_pass(b + 1)

    score(0, 0, s0, x0)

    def body(u, carry):
        score(u, 1, s1, x1)
        mix(u, 0, s0, x0)
        after_first(u)
        score(jnp.minimum(u + 1, UNITS - 1), 0, s0, x0)
        mix(u, 1, s1, x1)

        @pl.when(u == EARLY + ZN - 1)
        def _():
            for b in range(NQB):
                o, lse = partials(1, b)
                so[b, 0:DH, :] = o.astype(BF16)
                high = lse.astype(BF16).astype(F32)
                middle = (lse - high).astype(BF16).astype(F32)
                low = lse - high - middle
                row = lax.broadcasted_iota(jnp.int32, (16, QB), 0)
                so[b, DH:OROWS, :] = jnp.where(
                    row == 0, high, jnp.where(row == 1, middle, low)
                ).astype(BF16)
                o_first(b).start()

        return carry

    lax.fori_loop(0, UNITS, body, 0)

    for b in range(NQB):
        o_second(b).wait_recv()
        own, lse = partials(0, b)
        other = ro[b, 0:DH, :].astype(F32)
        rows = ro[b, DH:OROWS, :].astype(F32)
        lse_other = rows[0:1] + rows[1:2] + rows[2:3]
        largest = jnp.maximum(lse, lse_other)
        e_own, e_other = jnp.exp2(lse - largest), jnp.exp2(lse_other - largest)
        share = 1.0 / (e_own + e_other)
        result = own * (e_own * share) + other * (e_other * share)
        for h in range(QB // DH):
            c = b * QB + h * DH
            out_ref[:, c:c + DH] = result[:, h * DH:(h + 1) * DH].T.astype(BF16)

    for d in range(2):
        for s in range(1, ZN):
            kv_copy(d, s).wait_send()
    p_copy.wait_send()
    for b in range(NQB):
        q_first(b).wait_send()
        q_second(b).wait_send()
        o_first(b).wait_send()
        o_second(b).wait_send()


def solution(mesh):
    ny = mesh.shape["head"] // 2
    freqs = 500000.0 ** (-(2.0 * np.arange(HALF, dtype=np.float64)) / DH)
    freqs = np.broadcast_to(freqs.astype(np.float32)[:, None], (HALF, DH))

    def part(q_new, k_new, v_new, k_cache, v_cache, new_pos):
        dma = pltpu.SemaphoreType.DMA
        return pl.pallas_call(
            functools.partial(kernel, ny),
            out_shape=jax.ShapeDtypeStruct(q_new.shape, BF16),
            in_specs=[pl.BlockSpec(memory_space=pltpu.VMEM)] * 7,
            out_specs=pl.BlockSpec(memory_space=pltpu.VMEM),
            scratch_shapes=[
                pltpu.VMEM((2, NQB, DH, QB), BF16),
                pltpu.VMEM((NQB, DH, QB), BF16),
                pltpu.VMEM((ZN, 2, ROWS, DH), BF16),
                pltpu.VMEM((2, 8, DH), F32),
                pltpu.VMEM((2, NCB, OROWS, CB), F32),
                pltpu.VMEM((2, NCB, 1, CB), F32),
                pltpu.VMEM((2 * PART, CB), F32),
                pltpu.VMEM((2 * PART, CB), F32),
                pltpu.VMEM((1, CB), F32),
                pltpu.VMEM((1, CB), F32),
                pltpu.VMEM((NQB, OROWS, QB), BF16),
                pltpu.VMEM((NQB, OROWS, QB), BF16),
                pltpu.VMEM((NQB, OROWS, QB), BF16),
                dma((2, ZN - 1)), dma((2, ZN - 1)),
                dma((NQB,)), dma((NQB,)), dma((NQB,)), dma((NQB,)),
                dma((NQB,)), dma((NQB,)), dma((NQB,)), dma((NQB,)),
                dma, dma,
            ],
            compiler_params=pltpu.CompilerParams(
                collective_id=0, has_side_effects=True, vmem_limit_bytes=48 << 20
            ),
        )(q_new, k_new, v_new, k_cache, v_cache, new_pos.reshape(1, -1), jnp.asarray(freqs))

    rows = P(("rep", "ctx"), "head")
    return jax.shard_map(
        part,
        mesh=mesh,
        in_specs=(rows,) * 5 + (P(("rep", "ctx")),),
        out_specs=rows,
        check_vma=False,
    )
```

time: 478 us -> 65 us (0.14)
  waiting for transfers between devices: 307 us -> 0 us
  Pallas kernels: 0 us -> 59 us
  matrix products: 46.7 us -> 0 us
  blocking collectives: 44.1 us -> 0 us
  other arithmetic: 42.1 us -> 0 us
  local copies, waits for them, and re-layouts: 25.2 us -> 5.74 us
  starting transfers between devices: 11.2 us -> 0 us
    all_to_all x2 -> x0, waiting for transfers between devices: 168 us -> none  [the longest x1 162 us: body(): lax.all_to_all(out_buffer, 'ctx', split_axis=0, concat_axis=0, tiled=True)]
    ppermute x15 -> x0, waiting for transfers between devices: 139 us -> none  [passed_along(): return lax.ppermute(block, axis, route)]
    pallas_call x0 -> x1, Pallas kernels: none -> 59 us  [part(): pl.pallas_call(functools.partial(kernel, ny), out_shape=jax.ShapeDtypeStr...]
    dot_general x32 -> x0, matrix products: 46.7 us -> none  [the longest x16 29.9 us: attend_block(): jnp.einsum('kgqn,nkd->qkgd', weights, value_heads, preferred_element_type...]
    all_gather x1 -> x0, blocking collectives: 44.1 us -> none  [body(): every_pos = lax.all_gather(key_pos, 'ctx', axis=0, tiled=True)]
    reduce_sum x18 -> x0, other arithmetic: 26.2 us -> none  [the longest x16 21.1 us: attend_block(): total = jnp.sum(expo, axis=-1)]
    dynamic_update_slice x16 -> x0, local copies, waits for them, and re-layouts: 13.4 us -> none  [the longest x15 12.6 us: visit_block(): lax.dynamic_update_index_in_dim(out_buffer, part_out, anchor, 0)]
    all_to_all x2 -> x0, starting transfers between devices: 9.99 us -> none  [the longest x1 6.3 us: body(): lax.all_to_all(out_buffer, 'ctx', split_axis=0, concat_axis=0, tiled=True)]
  transfers between devices with their start and end apart: 17 -> 0, of which waited for: 17 -> 0; matrix products, arithmetic and copies ran while one was open for 19% -> 0% of each run, Pallas kernels for 0% -> 0%
where the time goes in v1:
time: 65 us; the launch traced here: 64.7 us
  Pallas kernels  59 us (91%)
  local copies, waits for them, and re-layouts  5.74 us (9%)
    pallas_call x1, Pallas kernels, part(): pl.pallas_call(functools.partial(kernel, ny), out_shape=jax.ShapeDtypeStr...  59 us
    unnamed x15, local copies, waits for them, and re-layouts  5.67 us

profile of v1, /device:TPU:8, one launch (start us, length us, event | category | flops | bytes accessed | tf_op | source)
XLA Modules:
  0.0 64.7 jit_solution(16220629235667603936)
XLA Ops:
  0.0 0.0 copy-start.6
  0.0 0.0 copy-start.3
  0.0 0.7 %copy-done.6 = f32[64]{0:T(128)S(1)} copy-done((f32[64]{0:T(128)S(1)}, f32[64]{0:T(128)}, u32[]{:S(2)}) %copy-start.6) | copy-done | bytes 280
  0.7 0.0 copy-start.5
  0.7 0.1 jit_solution_.3.freq_ref
  0.7 0.0 copy-done.3
  0.8 0.5 copy-done.5
  1.3 0.0 copy-start
  1.3 1.0 %copy-done = bf16[128,2048]{1,0:T(8,128)(2,1)S(1)} copy-done((bf16[128,2048]{1,0:T(8,128)(2,1)S(1)}, bf16[128,2048]{1,0:T(8,128)(2,1)}, u32[]{:S(2)}) %copy-start) | copy-done | bytes 524312
  2.4 0.0 copy-start.1
  2.4 0.9 %copy-done.1 = bf16[640,128]{1,0:T(8,128)(2,1)S(1)} copy-done((bf16[640,128]{1,0:T(8,128)(2,1)S(1)}, bf16[640,128]{1,0:T(8,128)(2,1)}, u32[]{:S(2)}) %copy-start.1) | copy-done | bytes 163864
  3.3 0.0 copy-start.2
  3.3 0.9 %copy-done.2 = bf16[640,128]{1,0:T(8,128)(2,1)S(1)} copy-done((bf16[640,128]{1,0:T(8,128)(2,1)S(1)}, bf16[640,128]{1,0:T(8,128)(2,1)}, u32[]{:S(2)}) %copy-start.2) | copy-done | bytes 163864
  4.2 0.0 copy-start.4
  4.2 0.8 %copy-done.4 = bf16[128,128]{1,0:T(8,128)(2,1)S(1)} copy-done((bf16[128,128]{1,0:T(8,128)(2,1)S(1)}, bf16[128,128]{1,0:T(8,128)(2,1)}, u32[]{:S(2)}) %copy-start.4) | copy-done | bytes 32792
  4.9 59.0 %shard_map.73 = bf16[128,2048]{1,0:T(8,128)(2,1)S(1)} custom-call(bf16[128,2048]{1,0:T(8,128)(2,1)S(1)} %copy-done, bf16[128,128]{1,0:T(8,128)(2,1)S(1)} %copy-done.3, bf16[128,128]{1,0:T(8,128)(2,1)S(1)} %copy-done.4, bf16[640,128]{1,0:T(8,128)(2,1)S(1)} %copy-done.1, bf16[640,128]{1,0:T(8,128)(2,1)S(1)} %copy-done.2, s32[1,128]{1,0:T(1,128)S(1)} %bitcast.1, ...), custom_call_target="tpu_custom_call" | custom-call | tf_op jit(solution)/shard_map/pallas_call | solution.py:295
  63.9 0.8 %copy.9 = bf16[128,2048]{1,0:T(8,128)(2,1)} copy(bf16[128,2048]{1,0:T(8,128)(2,1)S(1)} %shard_map.73) | data formatting | bytes 1048576
Async XLA Ops:
  0.0 0.7 %copy-start.6 = (f32[64]{0:T(128)S(1)}, f32[64]{0:T(128)}, u32[]{:S(2)}) copy-start(f32[64]{0:T(128)} %constant.2.clone) | copy-start | bytes 772
  0.0 0.8 %copy-start.3 = (bf16[128,128]{1,0:T(8,128)(2,1)S(1)}, bf16[128,128]{1,0:T(8,128)(2,1)}, u32[]{:S(2)}) copy-start(bf16[128,128]{1,0:T(8,128)(2,1)} %kn_ref.1) | copy-start | bytes 98308
  0.7 0.7 %copy-start.5 = (s32[128]{0:T(128)S(1)}, s32[128]{0:T(128)}, u32[]{:S(2)}) copy-start(s32[128]{0:T(128)} %param.12) | copy-start | bytes 1540
  1.3 1.0 %copy-start = (bf16[128,2048]{1,0:T(8,128)(2,1)S(1)}, bf16[128,2048]{1,0:T(8,128)(2,1)}, u32[]{:S(2)}) copy-start(bf16[128,2048]{1,0:T(8,128)(2,1)} %q_ref.1) | copy-start | bytes 1572868
  2.4 0.9 %copy-start.1 = (bf16[640,128]{1,0:T(8,128)(2,1)S(1)}, bf16[640,128]{1,0:T(8,128)(2,1)}, u32[]{:S(2)}) copy-start(bf16[640,128]{1,0:T(8,128)(2,1)} %kc_ref.1) | copy-start | bytes 491524
  3.3 0.9 %copy-start.2 = (bf16[640,128]{1,0:T(8,128)(2,1)S(1)}, bf16[640,128]{1,0:T(8,128)(2,1)}, u32[]{:S(2)}) copy-start(bf16[640,128]{1,0:T(8,128)(2,1)} %vc_ref.1) | copy-start | bytes 491524
  4.2 0.8 %copy-start.4 = (bf16[128,128]{1,0:T(8,128)(2,1)S(1)}, bf16[128,128]{1,0:T(8,128)(2,1)}, u32[]{:S(2)}) copy-start(bf16[128,128]{1,0:T(8,128)(2,1)} %vn_ref.1) | copy-start | bytes 98308

commit v2 on v1

v2 whole, which is shorter than its diff:
```python
import math

import jax
import jax.numpy as jnp
import numpy as np
from jax import lax
from jax.experimental import pallas as pl
from jax.experimental.pallas import tpu as pltpu
from jax.sharding import PartitionSpec as P

DH = 128
HALF = 64
F32 = jnp.float32
BF16 = jnp.bfloat16
MESH = pl.DeviceIdType.MESH
LOG2E = math.log2(math.e)
SCALE = LOG2E / math.sqrt(DH)
NEG = -1e30
CACHED = 10240
Q_ROWS = 128

ZN = 8
SIZES = (384, 256)
OLD = 640
NEW = 128
QB = 512
NQB = 4
CB = 1024
NCB = 2
ROWS = 2 * NEW + 16
OROWS = DH + 16
OWN, OTHER = 0, 1
UNITS = (
    [(OWN, b, s) for s in (0, 1) for b in (0, 1)]
    + [(OTHER, 0, 0), (OTHER, 0, 1), (OWN, 0, 2), (OWN, 1, 2), (OTHER, 0, 2)]
    + [(OWN, 0, 3), (OWN, 1, 3), (OTHER, 0, 3)]
    + [(OTHER, 1, s) for s in range(4)]
    + [(OTHER, b, s) for s in (4, 5) for b in (0, 1)]
    + [(OWN, b, 4) for b in (0, 1)]
    + [(OTHER, b, s) for s in (6, 7) for b in (0, 1)]
    + [(OWN, b, s) for s in (5, 6, 7) for b in (0, 1)]
)
GROUP = 4
LATE = 2 * ZN // GROUP


def mm(a, b):
    return lax.dot_general(
        a, b, (((1,), (0,)), ((), ())), preferred_element_type=F32
    )


def turn(x, cosine, sine):
    lower, upper = x[:HALF], x[HALF:]
    return jnp.concatenate(
        [lower * cosine - upper * sine, upper * cosine + lower * sine], axis=0
    )


def kernel(
    q_hbm, kn_hbm, vn_hbm, kc_hbm, vc_hbm, pos_hbm, freq_hbm, out_ref,
    q_ref, kn_ref, vn_ref, vc_ref, pos_ref, freq_ref, load_sem,
    qt, kva, kvb, nw, qp, acc, top, s0, s1, x0, x1, so, ro,
    kv_send, kv_recv, n_send, n_recv, q_send, q_recv, o_send, o_recv, w_send, w_recv,
):
    ctx = lax.axis_index("ctx")
    head = lax.axis_index("head")
    hi, z = ctx // ZN, ctx % ZN
    right = {"ctx": hi * ZN + (z + 1) % ZN, "head": head}
    left = {"ctx": hi * ZN + (z + ZN - 1) % ZN, "head": head}
    partner = {"ctx": (1 - hi) * ZN + z, "head": head}
    everyone = (right, left, partner)

    barrier = pltpu.get_barrier_semaphore()
    for other in everyone:
        pl.semaphore_signal(barrier, inc=1, device_id=other, device_id_type=MESH)

    def load(src, dst, i):
        return pltpu.make_async_copy(src, dst, load_sem.at[i])

    vc_load = load(vc_hbm, vc_ref, 0)
    kc_loads = [
        load(kc_hbm.at[pl.ds(0, SIZES[0])], kva.at[0, pl.ds(0, SIZES[0])], 1),
        load(kc_hbm.at[pl.ds(SIZES[0], SIZES[1])], kvb.at[0, pl.ds(0, SIZES[1])], 2),
    ]
    pos_load = load(pos_hbm, pos_ref, 3)
    freq_load = load(freq_hbm, freq_ref, 4)
    kn_load = load(kn_hbm, kn_ref, 5)
    vn_load = load(vn_hbm, vn_ref, 6)
    q_loads = [
        load(q_hbm.at[:, pl.ds(b * QB, QB)], q_ref.at[:, pl.ds(b * QB, QB)], 7 + b)
        for b in range(NQB)
    ]
    for one in (vc_load, *kc_loads, pos_load, freq_load, *q_loads, kn_load, vn_load):
        one.start()

    def remote(src, dst, send, recv, target):
        return pltpu.make_async_remote_copy(
            src_ref=src, dst_ref=dst, send_sem=send, recv_sem=recv,
            device_id=target, device_id_type=MESH,
        )

    def kv_copy(d, s):
        held = kva if s % 2 == 1 - d else kvb
        return remote(
            held.at[max(s - 2, 0)], held.at[s], kv_send.at[d, s - 1], kv_recv.at[d, s - 1],
            right if d == 0 else left,
        )

    def new_at(d, n):
        return 2 * n + d

    def n_copy(d, n):
        src = (n - 1 if d == 0 else 2 - n) if n <= 2 else new_at(d, n - 2)
        return remote(
            nw.at[src], nw.at[new_at(d, n)], n_send.at[d, n - 1], n_recv.at[d, n - 1],
            right if d == 0 else left,
        )

    def q_copy(b):
        return remote(qt.at[0, b], qt.at[1, b], q_send.at[b], q_recv.at[b], partner)

    def o_copy(b):
        return remote(so.at[b], ro.at[b], o_send.at[b], o_recv.at[b], partner)

    w_copy = remote(nw.at[0], nw.at[1], w_send, w_recv, partner)

    vc_load.wait()
    for t in range(3):
        kva[0, SIZES[0] + DH * t:SIZES[0] + DH * (t + 1), :] = (
            vc_ref[DH * t:DH * (t + 1), :].astype(F32).T.astype(BF16)
        )
    for t in range(2):
        r = SIZES[0] + DH * t
        kvb[0, SIZES[1] + DH * t:SIZES[1] + DH * (t + 1), :] = (
            vc_ref[r:r + DH, :].astype(F32).T.astype(BF16)
        )
    for one in kc_loads:
        one.wait()
    pl.semaphore_wait(barrier, len(everyone))
    for s in (1, 2):
        for d in range(2):
            kv_copy(d, s).start()

    pos_load.wait()
    freq_load.wait()
    positions = pos_ref[...].astype(F32)
    relative = positions - CACHED
    angle = freq_ref[:, 0:1] * positions
    cosine, sine = jnp.cos(angle), jnp.sin(angle)
    for b in range(NQB):
        q_loads[b].wait()
        for h in range(QB // DH):
            c = b * QB + h * DH
            x = q_ref[:, c:c + DH].astype(F32).T
            qt[0, b, :, h * DH:(h + 1) * DH] = turn(x, cosine, sine).astype(BF16)
        q_copy(b).start()
    acc[...] = jnp.zeros(acc.shape, F32)
    top[...] = jnp.full(top.shape, NEG, F32)
    qp[...] = jnp.broadcast_to(relative, (8, DH))
    kn_load.wait()
    vn_load.wait()
    nw[0, 0:NEW, :] = turn(kn_ref[...].astype(F32).T, cosine, sine).T.astype(BF16)
    nw[0, NEW:2 * NEW, :] = vn_ref[...].astype(F32).T.astype(BF16)
    number = [
        jnp.broadcast_to(relative[:, d * HALF:d * HALF + 1] * (1.0 / HALF), (8, DH))
        for d in range(2)
    ]
    nw[0, 2 * NEW:ROWS, :] = jnp.concatenate(number, axis=0).astype(BF16)

    def unit(u):
        found = []
        for field in zip(*UNITS):
            value = jnp.int32(field[0])
            for at in range(1, len(field)):
                if field[at] != field[at - 1]:
                    value = jnp.where(u >= at, field[at], value)
            found.append(value)
        return tuple(found)

    def queries(group, blk):
        return jnp.concatenate([qt[group, 2 * blk], qt[group, 2 * blk + 1]], axis=1)

    def score(at, s_ref, x_ref):
        group, blk, step = at
        q = queries(group, blk)
        sa = mm(kva[step, 0:SIZES[0], :], q) * SCALE
        sb = mm(kvb[step, 0:SIZES[1], :], q) * SCALE
        s_ref[0:SIZES[0], :] = sa
        s_ref[SIZES[0]:OLD, :] = sb
        x_ref[...] = jnp.maximum(
            jnp.max(sa, axis=0, keepdims=True), jnp.max(sb, axis=0, keepdims=True)
        )

    def score_new(i, blk, s_ref, x_ref):
        q = queries(0, blk)
        qpos = qp[0:1]
        best = None
        for j in range(GROUP):
            s = mm(nw[i * GROUP + j, 0:NEW, :], q) * SCALE
            number = nw[i * GROUP + j, 2 * NEW:ROWS, :].astype(F32)
            row = lax.broadcasted_iota(jnp.int32, (HALF, DH), 0).astype(F32)
            bias = jnp.concatenate(
                [
                    jnp.where(number[8 * d:8 * d + 1] * HALF + row <= qpos, 0.0, NEG)
                    for d in range(2)
                ],
                axis=0,
            )
            s = s + jnp.concatenate([bias] * (CB // DH), axis=1)
            s_ref[j * NEW:(j + 1) * NEW, :] = s
            m = jnp.max(s, axis=0, keepdims=True)
            best = m if best is None else jnp.maximum(best, m)
        x_ref[...] = best

    def mix_in(group, blk, s, x_ref, tiles):
        before = top[group, blk]
        after = jnp.maximum(before, x_ref[...])
        top[group, blk] = after
        fade = jnp.exp2(before - after)
        p = jnp.exp2(s - after).astype(BF16)
        v = jnp.concatenate(tiles, axis=1)
        v = jnp.concatenate([v, jnp.ones((16, v.shape[1]), BF16)], axis=0)
        acc[group, blk] = acc[group, blk] * fade + mm(v, p)

    def mix(at, s_ref, x_ref):
        group, blk, step = at
        tiles = [
            held[step, size + DH * t:size + DH * (t + 1), :]
            for held, size in ((kva, SIZES[0]), (kvb, SIZES[1]))
            for t in range(size // DH)
        ]
        mix_in(group, blk, s_ref[0:OLD, :], x_ref, tiles)

    def mix_new(i, blk, s_ref, x_ref):
        tiles = [nw[i * GROUP + j, NEW:2 * NEW, :] for j in range(GROUP)]
        mix_in(0, blk, s_ref[0:GROUP * NEW, :], x_ref, tiles)

    def kv_arrive(s):
        for d in range(2):
            kv_copy(d, s).wait_recv()
            if s + 2 < ZN:
                kv_copy(d, s + 2).start()

    def n_arrive(n):
        for d in range(2):
            n_copy(d, n).wait_recv()
            if n + 2 < ZN:
                n_copy(d, n + 2).start()

    def partials(group, b):
        blk, c = b // 2, (b % 2) * QB
        a = acc[group, blk, :, c:c + QB]
        total = a[DH:DH + 1]
        lse = top[group, blk, :, c:c + QB] + jnp.log(total) * LOG2E
        return a[:DH] / total, lse

    def finish(b):
        o, lse = partials(1, b)
        so[b, 0:DH, :] = o.astype(BF16)
        high = lse.astype(BF16).astype(F32)
        middle = (lse - high).astype(BF16).astype(F32)
        low = lse - high - middle
        row = lax.broadcasted_iota(jnp.int32, (16, QB), 0)
        so[b, DH:OROWS, :] = jnp.where(
            row == 0, high, jnp.where(row == 1, middle, low)
        ).astype(BF16)
        o_copy(b).start()

    def q_arrive(b):
        q_copy(b).wait_recv()

    def w_begin():
        w_copy.start()

    def n_begin():
        w_copy.wait_recv()
        for n in (1, 2):
            for d in range(2):
                n_copy(d, n).start()

    after = {
        0: [(kv_arrive, 1)],
        2: [(q_arrive, 0), (q_arrive, 1)],
        4: [(kv_arrive, 2)],
        7: [(kv_arrive, 3)],
        10: [(q_arrive, 2), (q_arrive, 3), (w_begin,)],
        11: [(kv_arrive, 4)],
        15: [(kv_arrive, 5), (n_begin,)],
        19: [(kv_arrive, 6)],
        22: [(kv_arrive, 7)],
        24: [(finish, 0), (finish, 1), (n_arrive, 1)],
        25: [(finish, 2), (finish, 3)],
        26: [(n_arrive, 2)],
        27: [(n_arrive, 3)],
        29: [(n_arrive, 4)],
    }

    def sync(u, odd):
        for at, actions in after.items():
            if at % 2 == odd:
                @pl.when(u == at)
                def _(actions=actions):
                    for action, *given in actions:
                        action(*given)

    score(UNITS[0], s0, x0)

    def body(i, now):
        u = 2 * i
        then = unit(u + 1)
        score(then, s1, x1)
        mix(now, s0, x0)
        sync(u, 0)
        now = unit(u + 2)
        score(now, s0, x0)
        mix(then, s1, x1)
        sync(u + 1, 1)
        return now

    first = tuple(jnp.int32(value) for value in UNITS[0])
    lax.fori_loop(0, len(UNITS) // 2 - 1, body, first)
    score(UNITS[-1], s1, x1)
    mix(UNITS[-2], s0, x0)
    n_arrive(5)
    score_new(0, 0, s0, x0)
    mix(UNITS[-1], s1, x1)

    def late(i, carry):
        score_new(i, 1, s1, x1)
        mix_new(i, 0, s0, x0)

        @pl.when(i == LATE - 2)
        def _():
            n_arrive(6)
            n_arrive(7)

        score_new(jnp.minimum(i + 1, LATE - 1), 0, s0, x0)
        mix_new(i, 1, s1, x1)
        return carry

    lax.fori_loop(0, LATE, late, 0)

    for b in range(NQB):
        o_copy(b).wait_recv()
        own, lse = partials(0, b)
        other = ro[b, 0:DH, :].astype(F32)
        rows = ro[b, DH:OROWS, :].astype(F32)
        lse_other = rows[0:1] + rows[1:2] + rows[2:3]
        largest = jnp.maximum(lse, lse_other)
        e_own, e_other = jnp.exp2(lse - largest), jnp.exp2(lse_other - largest)
        share = 1.0 / (e_own + e_other)
        result = own * (e_own * share) + other * (e_other * share)
        for h in range(QB // DH):
            c = b * QB + h * DH
            out_ref[:, c:c + DH] = result[:, h * DH:(h + 1) * DH].T.astype(BF16)

    for d in range(2):
        for s in range(1, ZN):
            kv_copy(d, s).wait_send()
            n_copy(d, s).wait_send()
    w_copy.wait_send()
    for b in range(NQB):
        q_copy(b).wait_send()
        o_copy(b).wait_send()


def solution(mesh):
    freqs = 500000.0 ** (-(2.0 * np.arange(HALF, dtype=np.float64)) / DH)
    table = np.zeros((HALF, DH), np.float32)
    table[:, :HALF] = freqs[:, None]

    def part(q_new, k_new, v_new, k_cache, v_cache, new_pos):
        dma = pltpu.SemaphoreType.DMA
        return pl.pallas_call(
            kernel,
            out_shape=jax.ShapeDtypeStruct(q_new.shape, BF16),
            in_specs=[pl.BlockSpec(memory_space=pltpu.HBM)] * 7,
            out_specs=pl.BlockSpec(memory_space=pltpu.VMEM),
            scratch_shapes=[
                pltpu.VMEM((Q_ROWS, NQB * QB), BF16),
                pltpu.VMEM((NEW, DH), BF16),
                pltpu.VMEM((NEW, DH), BF16),
                pltpu.VMEM((OLD, DH), BF16),
                pltpu.VMEM((1, Q_ROWS), jnp.int32),
                pltpu.VMEM((HALF, DH), F32),
                dma((7 + NQB,)),
                pltpu.VMEM((2, NQB, DH, QB), BF16),
                pltpu.VMEM((ZN, 2 * SIZES[0], DH), BF16),
                pltpu.VMEM((ZN, 2 * SIZES[1], DH), BF16),
                pltpu.VMEM((2 * ZN, ROWS, DH), BF16),
                pltpu.VMEM((8, DH), F32),
                pltpu.VMEM((2, NCB, OROWS, CB), F32),
                pltpu.VMEM((2, NCB, 1, CB), F32),
                pltpu.VMEM((OLD, CB), F32),
                pltpu.VMEM((OLD, CB), F32),
                pltpu.VMEM((1, CB), F32),
                pltpu.VMEM((1, CB), F32),
                pltpu.VMEM((NQB, OROWS, QB), BF16),
                pltpu.VMEM((NQB, OROWS, QB), BF16),
                dma((2, ZN - 1)), dma((2, ZN - 1)),
                dma((2, ZN - 1)), dma((2, ZN - 1)),
                dma((NQB,)), dma((NQB,)), dma((NQB,)), dma((NQB,)),
                dma, dma,
            ],
            compiler_params=pltpu.CompilerParams(
                collective_id=0, has_side_effects=True, vmem_limit_bytes=64 << 20
            ),
        )(q_new, k_new, v_new, k_cache, v_cache, new_pos.reshape(1, -1), jnp.asarray(table))

    rows = P(("rep", "ctx"), "head")
    return jax.shard_map(
        part,
        mesh=mesh,
        in_specs=(rows,) * 5 + (P(("rep", "ctx")),),
        out_specs=rows,
        check_vma=False,
    )
```

time: 65 us -> 58.8 us (0.905)
  local copies, waits for them, and re-layouts: 5.74 us -> 1.88 us
  Pallas kernels: 59 us -> 56.7 us
    unnamed x15 -> x1, local copies, waits for them, and re-layouts: 5.67 us -> 1.88 us
    pallas_call x1, Pallas kernels: 59 us -> 56.7 us  [part(): pl.pallas_call(kernel, out_shape=jax.ShapeDtypeStruct(q_new.shape, BF16),...]
where the time goes in v2:
time: 58.8 us; the launch traced here: 58.6 us
  Pallas kernels  56.7 us (96%)
  local copies, waits for them, and re-layouts  1.88 us (3%)
    pallas_call x1, Pallas kernels, part(): pl.pallas_call(kernel, out_shape=jax.ShapeDtypeStruct(q_new.shape, BF16),...  56.7 us
    unnamed x1, local copies, waits for them, and re-layouts  1.88 us

profile of v2, /device:TPU:8, one launch (start us, length us, event | category | flops | bytes accessed | tf_op | source)
XLA Modules:
  0.0 58.6 jit_solution(12843634697566367069)
XLA Ops:
  0.0 56.7 %shard_map.73 = bf16[128,2048]{1,0:T(8,128)(2,1)} custom-call(bf16[128,2048]{1,0:T(8,128)(2,1)} %q_hbm.1, bf16[128,128]{1,0:T(8,128)(2,1)} %kn_hbm.1, bf16[128,128]{1,0:T(8,128)(2,1)} %vn_hbm.1, bf16[640,128]{1,0:T(8,128)(2,1)} %kc_hbm.1, bf16[640,128]{1,0:T(8,128)(2,1)} %vc_hbm.1, s32[1,128]{1,0:T(1,128)} %bitcast.1, f32[64,128]{1,0:T(8,128)} %constant.2.clone.freq_hbm), custom_call_target="tpu_custom_call" | custom-call | tf_op jit(solution)/shard_map/pallas_call | solution.py:375
  56.7 1.9 %copy.9 = bf16[128,2048]{1,0:T(8,128)(2,1)} copy(bf16[128,2048]{1,0:T(8,128)(2,1)} %shard_map.73) | data formatting | bytes 1048576

commit v3 on v2

--- a/solution.py
+++ b/solution.py
@@ -58,10 +58,10 @@
 
 
 def kernel(
-    q_hbm, kn_hbm, vn_hbm, kc_hbm, vc_hbm, pos_hbm, freq_hbm, out_ref,
-    q_ref, kn_ref, vn_ref, vc_ref, pos_ref, freq_ref, load_sem,
+    q_hbm, kn_hbm, vn_hbm, kc_hbm, vc_hbm, pos_hbm, freq_hbm, out_hbm,
+    out_ref, out_sem, q_ref, kn_ref, vn_ref, vc_ref, pos_ref, freq_ref, load_sem,
     qt, kva, kvb, nw, qp, acc, top, s0, s1, x0, x1, so, ro,
-    kv_send, kv_recv, n_send, n_recv, q_send, q_recv, o_send, o_recv, w_send, w_recv,
+    k_send, k_recv, kv_send, kv_recv, n_send, n_recv, q_send, q_recv, o_send, o_recv, w_send, w_recv,
 ):
     ctx = lax.axis_index("ctx")
     head = lax.axis_index("head")
@@ -100,10 +100,26 @@
             device_id=target, device_id_type=MESH,
         )
 
+    def held_in(d, s):
+        return (kva, 0) if s % 2 == 1 - d else (kvb, 1)
+
+    def own_keys(d, s):
+        held, i = held_in(d, s)
+        return remote(
+            kc_hbm.at[pl.ds(i * SIZES[0], SIZES[i])], held.at[s, pl.ds(0, SIZES[i])],
+            k_send.at[d, s - 1], k_recv.at[d, s - 1], right if d == 0 else left,
+        )
+
     def kv_copy(d, s):
-        held = kva if s % 2 == 1 - d else kvb
+        held, i = held_in(d, s)
+        if s <= 2:
+            values = pl.ds(SIZES[i], SIZES[i])
+            return remote(
+                held.at[0, values], held.at[s, values], kv_send.at[d, s - 1],
+                kv_recv.at[d, s - 1], right if d == 0 else left,
+            )
         return remote(
-            held.at[max(s - 2, 0)], held.at[s], kv_send.at[d, s - 1], kv_recv.at[d, s - 1],
+            held.at[s - 2], held.at[s], kv_send.at[d, s - 1], kv_recv.at[d, s - 1],
             right if d == 0 else left,
         )
 
@@ -125,6 +141,9 @@
 
     w_copy = remote(nw.at[0], nw.at[1], w_send, w_recv, partner)
 
+    pl.semaphore_wait(barrier, len(everyone))
+    for d in range(2):
+        own_keys(d, 1).start()
     vc_load.wait()
     for t in range(3):
         kva[0, SIZES[0] + DH * t:SIZES[0] + DH * (t + 1), :] = (
@@ -135,12 +154,14 @@
         kvb[0, SIZES[1] + DH * t:SIZES[1] + DH * (t + 1), :] = (
             vc_ref[r:r + DH, :].astype(F32).T.astype(BF16)
         )
+    for d in range(2):
+        kv_copy(d, 1).start()
+    for d in range(2):
+        own_keys(d, 2).start()
+    for d in range(2):
+        kv_copy(d, 2).start()
     for one in kc_loads:
         one.wait()
-    pl.semaphore_wait(barrier, len(everyone))
-    for s in (1, 2):
-        for d in range(2):
-            kv_copy(d, s).start()
 
     pos_load.wait()
     freq_load.wait()
@@ -184,34 +205,27 @@
     def score(at, s_ref, x_ref):
         group, blk, step = at
         q = queries(group, blk)
-        sa = mm(kva[step, 0:SIZES[0], :], q) * SCALE
-        sb = mm(kvb[step, 0:SIZES[1], :], q) * SCALE
-        s_ref[0:SIZES[0], :] = sa
-        s_ref[SIZES[0]:OLD, :] = sb
-        x_ref[...] = jnp.maximum(
-            jnp.max(sa, axis=0, keepdims=True), jnp.max(sb, axis=0, keepdims=True)
-        )
+        k = jnp.concatenate(
+            [kva[step, 0:SIZES[0], :], kvb[step, 0:SIZES[1], :]], axis=0
+        )
+        s = mm(k, q) * SCALE
+        s_ref[0:OLD, :] = s
+        x_ref[...] = jnp.max(s, axis=0, keepdims=True)
 
     def score_new(i, blk, s_ref, x_ref):
         q = queries(0, blk)
         qpos = qp[0:1]
-        best = None
+        row = lax.broadcasted_iota(jnp.int32, (HALF, DH), 0).astype(F32)
+        bias = []
         for j in range(GROUP):
-            s = mm(nw[i * GROUP + j, 0:NEW, :], q) * SCALE
             number = nw[i * GROUP + j, 2 * NEW:ROWS, :].astype(F32)
-            row = lax.broadcasted_iota(jnp.int32, (HALF, DH), 0).astype(F32)
-            bias = jnp.concatenate(
-                [
-                    jnp.where(number[8 * d:8 * d + 1] * HALF + row <= qpos, 0.0, NEG)
-                    for d in range(2)
-                ],
-                axis=0,
-            )
-            s = s + jnp.concatenate([bias] * (CB // DH), axis=1)
-            s_ref[j * NEW:(j + 1) * NEW, :] = s
-            m = jnp.max(s, axis=0, keepdims=True)
-            best = m if best is None else jnp.maximum(best, m)
-        x_ref[...] = best
+            for d in range(2):
+                bias.append(jnp.where(number[8 * d:8 * d + 1] * HALF + row <= qpos, 0.0, NEG))
+        bias = jnp.concatenate(bias, axis=0)
+        k = jnp.concatenate([nw[i * GROUP + j, 0:NEW, :] for j in range(GROUP)], axis=0)
+        s = mm(k, q) * SCALE + jnp.concatenate([bias] * (CB // DH), axis=1)
+        s_ref[0:GROUP * NEW, :] = s
+        x_ref[...] = jnp.max(s, axis=0, keepdims=True)
 
     def mix_in(group, blk, s, x_ref, tiles):
         before = top[group, blk]
@@ -239,6 +253,8 @@
     def kv_arrive(s):
         for d in range(2):
             kv_copy(d, s).wait_recv()
+            if s <= 2:
+                own_keys(d, s).wait_recv()
             if s + 2 < ZN:
                 kv_copy(d, s + 2).start()
 
@@ -292,8 +308,7 @@
         24: [(finish, 0), (finish, 1), (n_arrive, 1)],
         25: [(finish, 2), (finish, 3)],
         26: [(n_arrive, 2)],
-        27: [(n_arrive, 3)],
-        29: [(n_arrive, 4)],
+        28: [(n_arrive, 3)],
     }
 
     def sync(u, odd):
@@ -322,27 +337,33 @@
     lax.fori_loop(0, len(UNITS) // 2 - 1, body, first)
     score(UNITS[-1], s1, x1)
     mix(UNITS[-2], s0, x0)
-    n_arrive(5)
+    n_arrive(4)
     score_new(0, 0, s0, x0)
     mix(UNITS[-1], s1, x1)
 
     def late(i, carry):
         score_new(i, 1, s1, x1)
         mix_new(i, 0, s0, x0)
+
+        @pl.when(i == 0)
+        def _():
+            n_arrive(5)
 
         @pl.when(i == LATE - 2)
         def _():
             n_arrive(6)
             n_arrive(7)
 
-        score_new(jnp.minimum(i + 1, LATE - 1), 0, s0, x0)
+        score_new(i + 1, 0, s0, x0)
         mix_new(i, 1, s1, x1)
         return carry
 
-    lax.fori_loop(0, LATE, late, 0)
-
-    for b in range(NQB):
-        o_copy(b).wait_recv()
+    def out_copy(b):
+        return pltpu.make_async_copy(
+            out_ref.at[:, pl.ds(b * QB, QB)], out_hbm.at[:, pl.ds(b * QB, QB)], out_sem.at[b]
+        )
+
+    def result(b):
         own, lse = partials(0, b)
         other = ro[b, 0:DH, :].astype(F32)
         rows = ro[b, DH:OROWS, :].astype(F32)
@@ -350,16 +371,33 @@
         largest = jnp.maximum(lse, lse_other)
         e_own, e_other = jnp.exp2(lse - largest), jnp.exp2(lse_other - largest)
         share = 1.0 / (e_own + e_other)
-        result = own * (e_own * share) + other * (e_other * share)
+        mixed = own * (e_own * share) + other * (e_other * share)
         for h in range(QB // DH):
             c = b * QB + h * DH
-            out_ref[:, c:c + DH] = result[:, h * DH:(h + 1) * DH].T.astype(BF16)
+            out_ref[:, c:c + DH] = mixed[:, h * DH:(h + 1) * DH].T.astype(BF16)
+        out_copy(b).start()
+
+    lax.fori_loop(0, LATE - 1, late, 0)
+    score_new(LATE - 1, 1, s1, x1)
+    mix_new(LATE - 1, 0, s0, x0)
+    for b in (0, 1):
+        o_copy(b).wait_recv()
+    mix_new(LATE - 1, 1, s1, x1)
+    result(0)
+    result(1)
+    for b in (2, 3):
+        o_copy(b).wait_recv()
+        result(b)
 
     for d in range(2):
         for s in range(1, ZN):
             kv_copy(d, s).wait_send()
+            if s <= 2:
+                own_keys(d, s).wait_send()
             n_copy(d, s).wait_send()
     w_copy.wait_send()
+    for b in range(NQB):
+        out_copy(b).wait()
     for b in range(NQB):
         q_copy(b).wait_send()
         o_copy(b).wait_send()
@@ -376,8 +414,10 @@
             kernel,
             out_shape=jax.ShapeDtypeStruct(q_new.shape, BF16),
             in_specs=[pl.BlockSpec(memory_space=pltpu.HBM)] * 7,
-            out_specs=pl.BlockSpec(memory_space=pltpu.VMEM),
+            out_specs=pl.BlockSpec(memory_space=pltpu.HBM),
             scratch_shapes=[
+                pltpu.VMEM((Q_ROWS, NQB * QB), BF16),
+                dma((NQB,)),
                 pltpu.VMEM((Q_ROWS, NQB * QB), BF16),
                 pltpu.VMEM((NEW, DH), BF16),
                 pltpu.VMEM((NEW, DH), BF16),
@@ -398,6 +438,7 @@
                 pltpu.VMEM((1, CB), F32),
                 pltpu.VMEM((NQB, OROWS, QB), BF16),
                 pltpu.VMEM((NQB, OROWS, QB), BF16),
+                dma((2, 2)), dma((2, 2)),
                 dma((2, ZN - 1)), dma((2, ZN - 1)),
                 dma((2, ZN - 1)), dma((2, ZN - 1)),
                 dma((NQB,)), dma((NQB,)), dma((NQB,)), dma((NQB,)),

time: 58.8 us -> 55.9 us (0.951)
  Pallas kernels: 56.7 us -> 53.8 us
    pallas_call x1, Pallas kernels: 56.7 us -> 53.8 us  [part(): pl.pallas_call(kernel, out_shape=jax.ShapeDtypeStruct(q_new.shape, BF16),...]
where the time goes in v3:
time: 55.9 us; the launch traced here: 55.7 us
  Pallas kernels  53.8 us (96%)
  local copies, waits for them, and re-layouts  1.88 us (3%)
    pallas_call x1, Pallas kernels, part(): pl.pallas_call(kernel, out_shape=jax.ShapeDtypeStruct(q_new.shape, BF16),...  53.8 us
    unnamed x1, local copies, waits for them, and re-layouts  1.88 us

profile of v3, /device:TPU:8, one launch (start us, length us, event | category | flops | bytes accessed | tf_op | source)
XLA Modules:
  0.0 55.7 jit_solution(9309966749374356554)
XLA Ops:
  0.0 53.8 %shard_map.73 = bf16[128,2048]{1,0:T(8,128)(2,1)} custom-call(bf16[128,2048]{1,0:T(8,128)(2,1)} %q_hbm.1, bf16[128,128]{1,0:T(8,128)(2,1)} %kn_hbm.1, bf16[128,128]{1,0:T(8,128)(2,1)} %vn_hbm.1, bf16[640,128]{1,0:T(8,128)(2,1)} %kc_hbm.1, bf16[640,128]{1,0:T(8,128)(2,1)} %vc_hbm.1, s32[1,128]{1,0:T(1,128)} %bitcast.1, f32[64,128]{1,0:T(8,128)} %constant.2.clone.freq_hbm), custom_call_target="tpu_custom_call" | custom-call | tf_op jit(solution)/shard_map/pallas_call | solution.py:413
  53.9 1.9 %copy.9 = bf16[128,2048]{1,0:T(8,128)(2,1)} copy(bf16[128,2048]{1,0:T(8,128)(2,1)} %shard_map.73) | data formatting | bytes 1048576

commit v4 on v3

--- a/solution.py
+++ b/solution.py
@@ -212,19 +212,19 @@
         s_ref[0:OLD, :] = s
         x_ref[...] = jnp.max(s, axis=0, keepdims=True)
 
-    def score_new(i, blk, s_ref, x_ref):
+    def score_new(i, blk, s_ref, x_ref, first=0, count=GROUP):
         q = queries(0, blk)
         qpos = qp[0:1]
         row = lax.broadcasted_iota(jnp.int32, (HALF, DH), 0).astype(F32)
         bias = []
-        for j in range(GROUP):
+        for j in range(first, first + count):
             number = nw[i * GROUP + j, 2 * NEW:ROWS, :].astype(F32)
             for d in range(2):
                 bias.append(jnp.where(number[8 * d:8 * d + 1] * HALF + row <= qpos, 0.0, NEG))
         bias = jnp.concatenate(bias, axis=0)
-        k = jnp.concatenate([nw[i * GROUP + j, 0:NEW, :] for j in range(GROUP)], axis=0)
+        k = jnp.concatenate([nw[i * GROUP + j, 0:NEW, :] for j in range(first, first + count)], axis=0)
         s = mm(k, q) * SCALE + jnp.concatenate([bias] * (CB // DH), axis=1)
-        s_ref[0:GROUP * NEW, :] = s
+        s_ref[0:count * NEW, :] = s
         x_ref[...] = jnp.max(s, axis=0, keepdims=True)
 
     def mix_in(group, blk, s, x_ref, tiles):
@@ -246,9 +246,9 @@
         ]
         mix_in(group, blk, s_ref[0:OLD, :], x_ref, tiles)
 
-    def mix_new(i, blk, s_ref, x_ref):
-        tiles = [nw[i * GROUP + j, NEW:2 * NEW, :] for j in range(GROUP)]
-        mix_in(0, blk, s_ref[0:GROUP * NEW, :], x_ref, tiles)
+    def mix_new(i, blk, s_ref, x_ref, first=0, count=GROUP):
+        tiles = [nw[i * GROUP + j, NEW:2 * NEW, :] for j in range(first, first + count)]
+        mix_in(0, blk, s_ref[0:count * NEW, :], x_ref, tiles)
 
     def kv_arrive(s):
         for d in range(2):
@@ -349,11 +349,6 @@
         def _():
             n_arrive(5)
 
-        @pl.when(i == LATE - 2)
-        def _():
-            n_arrive(6)
-            n_arrive(7)
-
         score_new(i + 1, 0, s0, x0)
         mix_new(i, 1, s1, x1)
         return carry
@@ -377,12 +372,23 @@
             out_ref[:, c:c + DH] = mixed[:, h * DH:(h + 1) * DH].T.astype(BF16)
         out_copy(b).start()
 
-    lax.fori_loop(0, LATE - 1, late, 0)
-    score_new(LATE - 1, 1, s1, x1)
-    mix_new(LATE - 1, 0, s0, x0)
+    lax.fori_loop(0, LATE - 2, late, 0)
+    end, half = LATE - 1, GROUP // 2
+    score_new(end - 1, 1, s1, x1)
+    mix_new(end - 1, 0, s0, x0)
+    n_arrive(6)
+    score_new(end, 0, s0, x0, 0, half)
+    mix_new(end - 1, 1, s1, x1)
+    score_new(end, 1, s1, x1, 0, half)
+    mix_new(end, 0, s0, x0, 0, half)
+    n_arrive(7)
+    score_new(end, 0, s0, x0, half, half)
+    mix_new(end, 1, s1, x1, 0, half)
+    score_new(end, 1, s1, x1, half, half)
+    mix_new(end, 0, s0, x0, half, half)
     for b in (0, 1):
         o_copy(b).wait_recv()
-    mix_new(LATE - 1, 1, s1, x1)
+    mix_new(end, 1, s1, x1, half, half)
     result(0)
     result(1)
     for b in (2, 3):

time: 55.9 us -> 55.1 us (0.986)
  Pallas kernels: 53.8 us -> 53.1 us
    pallas_call x1, Pallas kernels: 53.8 us -> 53.1 us  [part(): pl.pallas_call(kernel, out_shape=jax.ShapeDtypeStruct(q_new.shape, BF16),...]
where the time goes in v4:
time: 55.1 us; the launch traced here: 54.9 us
  Pallas kernels  53.1 us (96%)
  local copies, waits for them, and re-layouts  1.88 us (3%)
    pallas_call x1, Pallas kernels, part(): pl.pallas_call(kernel, out_shape=jax.ShapeDtypeStruct(q_new.shape, BF16),...  53.1 us
    unnamed x1, local copies, waits for them, and re-layouts  1.88 us

profile of v4, /device:TPU:8, one launch (start us, length us, event | category | flops | bytes accessed | tf_op | source)
XLA Modules:
  0.0 54.9 jit_solution(10801209912174960736)
XLA Ops:
  0.0 53.1 %shard_map.73 = bf16[128,2048]{1,0:T(8,128)(2,1)} custom-call(bf16[128,2048]{1,0:T(8,128)(2,1)} %q_hbm.1, bf16[128,128]{1,0:T(8,128)(2,1)} %kn_hbm.1, bf16[128,128]{1,0:T(8,128)(2,1)} %vn_hbm.1, bf16[640,128]{1,0:T(8,128)(2,1)} %kc_hbm.1, bf16[640,128]{1,0:T(8,128)(2,1)} %vc_hbm.1, s32[1,128]{1,0:T(1,128)} %bitcast.1, f32[64,128]{1,0:T(8,128)} %constant.2.clone.freq_hbm), custom_call_target="tpu_custom_call" | custom-call | tf_op jit(solution)/shard_map/pallas_call | solution.py:419
  53.1 1.9 %copy.9 = bf16[128,2048]{1,0:T(8,128)(2,1)} copy(bf16[128,2048]{1,0:T(8,128)(2,1)} %shard_map.73) | data formatting | bytes 1048576

commit v5 on v4

--- a/solution.py
+++ b/solution.py
@@ -1,3 +1,4 @@
+import functools
 import math
 
 import jax
@@ -312,8 +313,11 @@
     }
 
     def sync(u, odd):
-        for at, actions in after.items():
-            if at % 2 == odd:
+        table = {at: actions for at, actions in after.items() if at % 2 == odd}
+
+        @pl.when(functools.reduce(jnp.logical_or, [u == at for at in table]))
+        def _():
+            for at, actions in table.items():
                 @pl.when(u == at)
                 def _(actions=actions):
                     for action, *given in actions:

time: 55.1 us -> 54.9 us (level)
  no operation moved by 1% of the time
where the time goes in v5:
time: 54.9 us; the launch traced here: 54.7 us
  Pallas kernels  52.8 us (96%)
  local copies, waits for them, and re-layouts  1.88 us (3%)
    pallas_call x1, Pallas kernels, part(): pl.pallas_call(kernel, out_shape=jax.ShapeDtypeStruct(q_new.shape, BF16),...  52.8 us
    unnamed x1, local copies, waits for them, and re-layouts  1.88 us

profile of v5, /device:TPU:8, one launch (start us, length us, event | category | flops | bytes accessed | tf_op | source)
XLA Modules:
  0.0 54.7 jit_solution(2610967749281724365)
XLA Ops:
  0.0 52.8 %shard_map.73 = bf16[128,2048]{1,0:T(8,128)(2,1)} custom-call(bf16[128,2048]{1,0:T(8,128)(2,1)} %q_hbm.1, bf16[128,128]{1,0:T(8,128)(2,1)} %kn_hbm.1, bf16[128,128]{1,0:T(8,128)(2,1)} %vn_hbm.1, bf16[640,128]{1,0:T(8,128)(2,1)} %kc_hbm.1, bf16[640,128]{1,0:T(8,128)(2,1)} %vc_hbm.1, s32[1,128]{1,0:T(1,128)} %bitcast.1, f32[64,128]{1,0:T(8,128)} %constant.2.clone.freq_hbm), custom_call_target="tpu_custom_call" | custom-call | tf_op jit(solution)/shard_map/pallas_call | solution.py:423
  52.8 1.9 %copy.9 = bf16[128,2048]{1,0:T(8,128)(2,1)} copy(bf16[128,2048]{1,0:T(8,128)(2,1)} %shard_map.73) | data formatting | bytes 1048576
